TPU v7x, 32 devices: a whole 2x2x4 slice. The times are simulated.
32 devices in a mesh: box: 8 (over y, x, core), dir: 4 (over z).
Axes of the slice: x: 2, y: 2, z: 4, core: 2. Of those that a mesh axis runs over, the one named last changes fastest.
Arguments:
- currents: bfloat16 [512, 8, 128], P(('box', 'dir')), may hold values from -6 to 6
- positions: bfloat16 [512, 3, 128], P(('box', 'dir')), may hold values from -2 to 2
- radiation: bfloat16 [128, 256], replicated, may hold values from -0.5 to 0.5
- interp_index: int32 [512, 4], replicated, may hold values from 0 to 127
- interp_weight: float32 [512, 4], replicated, may hold values from -3 to 3
- child_phase: float32 [8, 512], replicated, may hold values from -3.140625 to 3.140625
- near_src: int32 [512, 27], P(('box', 'dir')), may hold values from 0 to 511, as said below
- trans_src: int32 [64, 32], P('box'), may hold values from 0 to 63, as said below
- trans_id: int32 [64, 32], P('box'), may hold values from 0 to 315
- trans_count: int32 [64], P('box'), may hold values from 16 to 32, as said below
- trans_table: float32 [316, 2, 512], replicated, may hold values from -0.009 to 0.009
Outputs:
- field: float32 [512, 8, 128], P(('box', 'dir'))
Inputs may be any that keep to these rules, and one draw needn't show every extreme that they name: `near_src`: entry 0 of row i is i itself; every entry lies in the block of 16 boxes that holds i or in a block beside it. `trans_src`: every entry lies in the block of 8 parents that holds the row's parent or in a block beside it. Entries at and after trans_count are ignored; some parent in every block of 8 has 32.
All inputs are finite; a program needn't handle non-finite values.
Results may differ from a plain program's by a relative error of at most 0.0045.
Values may be sent and summed in bfloat16 or wider, within the bound.
No kernel may reach another device: no remote copies, remote signals or barrier semaphores. Data moves between devices by JAX's collectives and lax.ppermute only.
A program may use at most 64 MiB of HBM per device.

v0:
```python
import functools
import math

import jax
import jax.numpy as jnp
from jax import lax
from jax.experimental import pallas as pl
from jax.experimental.pallas import tpu as pltpu
from jax.sharding import PartitionSpec as P

F32 = jnp.float32
BF16 = jnp.bfloat16

WAVENUMBER = 4.0
OFFSET = 0.5
TURN = WAVENUMBER / (2.0 * math.pi)
S0, S1, S2 = (-0.08849679958812066, 0.5822236432316782, -1.1456733260321648)
LEAD = -70.99877392901621
ROUNDER = 12582912.0
ITEMS = 4
ROWS = 32
OWN_MOST = 4


def round_up(value, step):
    return -(-value // step) * step


def swapped(x, axis, pairs):
    return lax.ppermute(x, axis, [way for i, j in pairs for way in ((i, j), (j, i))])


def split3(x):
    high = x.astype(BF16).astype(F32)
    rest = x - high
    mid = rest.astype(BF16).astype(F32)
    return high, mid, rest - mid


def nt_dot(a, b):
    return lax.dot_general(a, b, (((1,), (1,)), ((), ())), preferred_element_type=F32)


def nn_dot(a, b):
    return jnp.dot(a, b, preferred_element_type=F32)


def code_shifts(boxes, entries):
    count_bits = entries.bit_length()
    box_bits = (boxes - 1).bit_length()
    return count_bits, count_bits + box_bits, 2 * count_bits + box_bits, 2 * (count_bits + box_bits)


def list_places(boxes, entries):
    gap = 6 * ITEMS
    most = OWN_MOST * boxes
    cross = most + gap
    end = cross + boxes * ((boxes + 1) // 2) + gap + (boxes * entries + 3 * boxes) // 2 + gap + 3
    return most, cross, round_up(end, 128)


def list_items(near_src, block, here, size):
    boxes, entries = near_src.shape
    most, cross_start, length = list_places(boxes, entries)
    first_box, second_count, second_box, source = code_shifts(boxes, entries)
    lanes = round_up(3 * boxes, 128)
    odd = (here & 1) == 1
    edge = (here == 0) | (here == size - 1)
    local = near_src - block * boxes
    below = local + jnp.where(odd, 2 * boxes, 3 * boxes)
    above = local + jnp.where(odd, boxes, 0)
    local = jnp.where(local < 0, below, jnp.where(local >= boxes, above, local))
    lane = lax.broadcasted_iota(jnp.int32, (boxes, lanes), 1)
    box = lax.broadcasted_iota(jnp.int32, (boxes, lanes), 0)
    count = jnp.zeros((boxes, lanes), jnp.int32)
    for e in range(entries):
        count = count + (local[:, e : e + 1] == lane).astype(jnp.int32)
    present = count > 0
    flags = present.astype(F32)
    box_row = lax.broadcasted_iota(jnp.int32, (boxes, boxes), 0)
    box_col = lax.broadcasted_iota(jnp.int32, (boxes, boxes), 1)
    rank = nn_dot((box_col < box_row).astype(F32).astype(BF16), flags.astype(BF16)).astype(jnp.int32)
    items = (jnp.sum(flags, axis=0, keepdims=True).astype(jnp.int32) + 1) >> 1
    from_own = lane < boxes
    from_cross = (lane >= 2 * boxes) & edge
    own_items = jnp.where(from_own[:1], items, 0).astype(F32)
    cross_items = jnp.where(from_cross[:1], items, 0).astype(F32)
    other_items = jnp.where(from_own[:1] | from_cross[:1], 0, items).astype(F32)
    row = lax.broadcasted_iota(jnp.int32, (lanes, lanes), 0)
    col = lax.broadcasted_iota(jnp.int32, (lanes, lanes), 1)
    ahead = (row < col).astype(F32).astype(BF16)
    lists = jnp.concatenate([own_items, other_items, cross_items, jnp.zeros((5, lanes), F32)], axis=0)
    offset = nn_dot(lists.astype(BF16), ahead).astype(jnp.int32)
    own_total = jnp.sum(own_items, axis=1, keepdims=True).astype(jnp.int32)
    other_total = jnp.sum(other_items, axis=1, keepdims=True).astype(jnp.int32)
    cross_total = jnp.sum(cross_items, axis=1, keepdims=True).astype(jnp.int32)
    half = rank >> 1
    own_place = offset[0:1] + half
    other_place = jnp.where(from_own, other_total + own_place - most, offset[1:2] + half)
    place = jnp.where(from_own & (own_place < most), own_place, (length - 4) - other_place)
    place = jnp.where(from_cross, cross_start + offset[2:3] + half, place)
    place = jnp.where(present, place, -1)
    code = jnp.where(
        (rank & 1) == 0,
        (lane << source) | (box << first_box) | count,
        (box << second_box) | (count << second_count),
    )
    place_t = place.T
    code_t = code.T
    rows = 3 * boxes
    slot = lax.broadcasted_iota(jnp.int32, (rows, length), 1)
    found = jnp.zeros((rows, length), jnp.int32)
    for i in range(boxes):
        hit = place_t[:rows, i : i + 1] == slot
        found = found + jnp.where(hit, code_t[:rows, i : i + 1], 0)
    listed = jnp.sum(found, axis=0, keepdims=True)
    other_total = other_total + jnp.maximum(own_total - most, 0)
    own_total = jnp.minimum(own_total, most)
    at = lax.broadcasted_iota(jnp.int32, (1, length), 1)
    listed = jnp.where(at == length - 3, own_total, listed)
    return jnp.where(at == length - 2, other_total, jnp.where(at == length - 1, cross_total, listed))


def start_all(copies, sems):
    started = [pltpu.make_async_copy(src, dst, sems.at[k]) for k, (src, dst) in enumerate(copies)]
    for copy in started:
        copy.start()
    return started


def wait_all(started):
    for copy in started:
        copy.wait()


def outgoing_kernel(
    x_hbm, pos_hbm, rad_hbm, idx_hbm, wgt_hbm, phase_hbm, packet_ref, spectra_ref, imat_ref, cos_ref, sin_ref, rad_ref,
    x_ref, pos_ref, idx_ref, wgt_ref, phase_ref, sems
):
    wait_all(
        start_all(
            (
                (x_hbm, x_ref),
                (pos_hbm, pos_ref),
                (rad_hbm, rad_ref),
                (idx_hbm, idx_ref),
                (wgt_hbm, wgt_ref),
                (phase_hbm, phase_ref),
            ),
            sems,
        )
    )
    leaf_dirs, parent_dirs = imat_ref.shape
    boxes, waves, width = x_ref.shape
    chunks = parent_dirs // 128
    x = x_ref[...].astype(F32)
    planes = pos_ref[...].astype(F32)
    at = lax.broadcasted_iota(jnp.int32, (boxes, 16 - waves, width), 1)
    pos = jnp.zeros((boxes, 16 - waves, width), F32)
    for axis in range(3):
        pos = jnp.where(at == axis, planes[axis][:, None, :], pos)
    packet_ref[:boxes] = jnp.concatenate([x, pos], axis=1).astype(BF16)
    column = lax.broadcasted_iota(jnp.int32, (leaf_dirs, parent_dirs), 0)
    imat = jnp.zeros((leaf_dirs, parent_dirs), F32)
    for s in range(idx_ref.shape[0]):
        imat = imat + jnp.where(idx_ref[s : s + 1, :] == column, wgt_ref[s : s + 1, :], 0.0)
    imat = imat.astype(BF16)
    imat_ref[...] = imat
    cos_phase = jnp.cos(phase_ref[...])
    sin_phase = jnp.sin(phase_ref[...])
    cos_ref[...] = cos_phase
    sin_ref[...] = sin_phase
    leaf = nn_dot(x.reshape(boxes * waves, width).astype(BF16), rad_ref[...]).astype(BF16)
    up_re = nn_dot(leaf[:, :leaf_dirs], imat)
    up_im = nn_dot(leaf[:, leaf_dirs:], imat)
    for q in range(boxes // 8):
        re = jnp.zeros((waves, parent_dirs), F32)
        im = jnp.zeros((waves, parent_dirs), F32)
        for c in range(8):
            at = (q * 8 + c) * waves
            ure = up_re[at : at + waves]
            uim = up_im[at : at + waves]
            re = re + (cos_phase[c : c + 1] * ure - sin_phase[c : c + 1] * uim)
            im = im + (sin_phase[c : c + 1] * ure + cos_phase[c : c + 1] * uim)
        both = jnp.concatenate([re, im], axis=0).astype(BF16)
        for k in range(chunks):
            part = both[:, k * 128 : (k + 1) * 128]
            packet_ref[boxes + q * chunks + k] = part
            spectra_ref[q * chunks + k] = part


def carries_packet(step):
    return step & (step + 1) == 0


def group_kernel(own_ref, *refs):
    *step_refs, _, group_ref = refs
    size = lax.axis_size("dir")
    rows = own_ref.shape[0]
    here = lax.axis_index("dir")
    group_ref[pl.ds(here * rows, rows)] = own_ref[...]
    for step, ref in enumerate(step_refs, 1):
        group_ref[pl.ds((here ^ step) * rows, rows)] = ref[ref.shape[0] - rows :]
    group_ref[size * rows :] = step_refs[-1][: step_refs[-1].shape[0] - rows]


def features(pos):
    scale = TURN * TURN
    norm = split3(scale * jnp.sum(pos * pos, axis=1, keepdims=True))
    at = lax.broadcasted_iota(jnp.int32, pos.shape, 1)
    first = jnp.where(at < 3, pos, 1.0)
    first = jnp.where(at == 3, norm[0], jnp.where(at == 4, norm[1], jnp.where(at == 5, norm[2], first)))
    second = jnp.where(at == 3, 1.0, pos + pltpu.roll(pos, 4, 1))
    source = jnp.concatenate([first, second], axis=1).astype(BF16)
    cross = split3((-2.0 * scale) * pos)
    first = jnp.where(at < 3, cross[0], 1.0)
    first = jnp.where(at == 6, norm[0], jnp.where(at == 7, norm[1], first))
    second = jnp.where(at == 3, norm[2], cross[1] + pltpu.roll(cross[2], 4, 1))
    return source, jnp.concatenate([first, second], axis=1).astype(BF16)


def turn_sources(source, src_ref, start):
    boxes, rows, width = source.shape
    eye = lax.broadcasted_iota(jnp.int32, (width, width), 0) == lax.broadcasted_iota(jnp.int32, (width, width), 1)
    turned = nt_dot(eye.astype(F32).astype(BF16), source.reshape(boxes * rows, width))
    for b in range(boxes):
        at = b * rows
        lanes = turned[:, at // 128 * 128 : at // 128 * 128 + 128]
        if at % 128:
            lanes = pltpu.roll(lanes, 128 - at % 128, 1)
        src_ref[start + b] = lanes.astype(BF16)


def near_sum(entries, total, item_at, first_source, src_ref, win_ref, obs_ref, out_ref, scratch):
    u0_ref, u1_ref, t0_ref, t1_ref = scratch
    boxes, waves, width = out_ref.shape
    first_box, second_count, second_box, source = code_shifts(boxes, entries)
    t1_ref[...] = jnp.zeros(t1_ref.shape, BF16)

    def field(code, low, high):
        return (code >> low) & ((1 << (high - low)) - 1)

    def source_at(code):
        return jnp.maximum((code >> source) - first_source, 0) if first_source else code >> source

    def distances(chunk, g, u_ref):
        code = item_at(chunk * ITEMS + g)
        observers = [obs_ref[field(code, first_box, second_count)], obs_ref[field(code, second_box, source)]]
        u_ref[g] = nn_dot(src_ref[source_at(code)][:, :16], jnp.concatenate(observers, axis=1))

    def tile(g, u_ref, t_ref):
        for at in range(0, width, ROWS):
            v = jnp.maximum(u_ref[g, at : at + ROWS], 1e-12)
            q = v * lax.rsqrt(v)
            t = q - ((q + ROUNDER) - ROUNDER)
            x = 0.25 - jnp.abs(t)
            z = x * x
            cosine = x * (((z + S2) * z + S1) * z + S0)
            t_ref[g, at : at + ROWS] = (cosine * pltpu.reciprocal(q + OFFSET * TURN, approx=True)).astype(BF16)

    def product(chunk, g, t_ref):
        code = item_at(chunk * ITEMS + g)
        got = nn_dot(win_ref[source_at(code)], t_ref[g])
        out_ref[field(code, first_box, second_count)] += field(code, 0, first_box).astype(F32) * got[:waves, :width]
        out_ref[field(code, second_box, source)] += field(code, second_count, second_box).astype(F32) * got[:waves, width:]

    def stages(chunk, u_ref, next_u_ref, t_ref, last_t_ref):
        for g in range(ITEMS):
            distances(chunk + 1, g, next_u_ref)
            product(jnp.maximum(chunk - 1, 0), g, last_t_ref)
            tile(g, u_ref, t_ref)

    rounds = (total + (2 * ITEMS - 1)) // (2 * ITEMS)
    for g in range(ITEMS):
        distances(0, g, u0_ref)

    def body(k, carry):
        stages(2 * k, u0_ref, u1_ref, t0_ref, t1_ref)
        stages(2 * k + 1, u1_ref, u0_ref, t1_ref, t0_ref)
        return carry

    lax.fori_loop(0, rounds, body, 0)
    for g in range(ITEMS):
        product(jnp.maximum(2 * rounds - 1, 0), g, t1_ref)


def own_near_kernel(
    own_ref, near_hbm, src_hbm, id_hbm, count_hbm, table_hbm, out_ref, items_ref, obs_ref, src_ref, gain_ref, near_ref,
    list_ref, trans_src_ref, trans_id_ref, trans_count_ref, rows_ref, *scratch
):
    *scratch, sems = scratch
    boxes, waves, width = out_ref.shape
    entries = near_ref.shape[1]
    length = items_ref.shape[1]
    parents, window = gain_ref.shape[:2]
    listed = src_hbm.shape[1]
    near_copy, *list_copies = start_all(
        (
            (near_hbm, near_ref),
            (src_hbm, trans_src_ref),
            (id_hbm, trans_id_ref),
            (count_hbm, trans_count_ref),
        ),
        sems,
    )
    out_ref[...] = jnp.zeros(out_ref.shape, F32)
    gain_ref[...] = jnp.zeros(gain_ref.shape, F32)
    source, observer = features(own_ref[:boxes].astype(F32)[:, 8:16, :])
    turn_sources(source, src_ref, 0)
    obs_ref[...] = observer
    near_copy.wait()
    block = lax.axis_index(("box", "dir"))
    items_ref[...] = list_items(near_ref[...], block, lax.axis_index("dir"), lax.axis_size("dir"))
    send_list = pltpu.make_async_copy(items_ref, list_ref, sems.at[0])
    send_list.start()
    wait_all(list_copies)
    row0 = lax.axis_index("dir") * parents
    for q in range(parents):
        for e in range(listed):
            pltpu.make_async_copy(
                table_hbm.at[trans_id_ref[row0 + q, e]], rows_ref.at[q * listed + e], sems.at[1]
            ).start()
    send_list.wait()
    near_sum(entries, list_ref[0, length - 3], lambda k: list_ref[0, k], 0, src_ref, own_ref, obs_ref, out_ref, scratch)
    pltpu.make_async_copy(rows_ref, rows_ref, sems.at[1]).wait()
    first = (lax.axis_index("box") - 1) * (window // 3)
    for q in range(parents):
        for e in range(listed):
            live = (e < trans_count_ref[row0 + q]).astype(F32)
            s = jnp.clip(trans_src_ref[row0 + q, e] - first, 0, window - 1)
            gain_ref[q, s] += rows_ref[q * listed + e] * live


def group_near_kernel(entries, items_ref, own_ref, *refs):
    *step_refs, obs_ref, own_src_ref, sum_ref, out_ref, win_ref, src_ref, u0_ref, u1_ref, t0_ref, t1_ref = refs
    boxes, waves, width = out_ref.shape
    length = items_ref.shape[1]
    here = lax.axis_index("dir")
    other_side = jnp.where((here & 1) == 0, here - 1, here + 1)

    def take(ref, part):
        win_ref[part * boxes : (part + 1) * boxes] = ref[:boxes]
        source, _ = features(ref[:boxes].astype(F32)[:, 8:16, :])
        turn_sources(source, src_ref, part * boxes)

    win_ref[:boxes] = own_ref[:boxes]
    src_ref[:boxes] = own_src_ref[...]
    take(step_refs[0], 1)
    for k, ref in enumerate(step_refs[1:], 2):
        pl.when((here ^ ((1 << k) - 1)) == other_side)(functools.partial(take, ref, 2))
    out_ref[...] = sum_ref[...]
    near_sum(
        entries,
        items_ref[0, length - 2],
        lambda k: items_ref[0, length - 4 - k],
        0,
        src_ref,
        win_ref,
        obs_ref,
        out_ref,
        (u0_ref, u1_ref, t0_ref, t1_ref),
    )


def incoming_kernel(
    entries, items_ref, even_ref, own_ref, odd_ref, gain_ref, cos_ref, sin_ref, imat_ref, rad_ref, obs_ref, near_ref, out_ref,
    sum_ref, win_ref, src_ref, down_re_ref, down_im_ref, *scratch
):
    parents, window, _, parent_dirs = gain_ref.shape
    boxes, waves, width = near_ref.shape
    chunks = parent_dirs // 128
    group = window // 3
    cross_start = list_places(boxes, entries)[1]
    cross_total = items_ref[0, items_ref.shape[1] - 1]
    odd_box = lax.axis_index("box") & 1
    sum_ref[...] = near_ref[...]

    @pl.when(cross_total > 0)
    def _():
        first = jnp.where(lax.axis_index("dir") == 0, 1, 0)

        @pl.when(first == odd_box)
        def _():
            win_ref[...] = even_ref[even_ref.shape[0] - boxes :]

        @pl.when(first != odd_box)
        def _():
            win_ref[...] = odd_ref[odd_ref.shape[0] - boxes :]

        source, _ = features(win_ref[...].astype(F32)[:, 8:16, :])
        turn_sources(source, src_ref, 0)
        near_sum(
            entries,
            cross_total,
            lambda k: items_ref[0, cross_start + k],
            2 * boxes,
            src_ref,
            win_ref,
            obs_ref,
            sum_ref,
            scratch,
        )

    cos_phase = cos_ref[...]
    sin_phase = sin_ref[...]
    sums = tuple(jnp.zeros((waves, 128), F32) for _ in range(parents * chunks * 2))
    for part, ref in ((2 - 2 * odd_box, even_ref), (1, own_ref), (2 * odd_box, odd_ref)):

        def add_source(s, sums, part=part, ref=ref):
            sums = list(sums)
            gains = [gain_ref[q, part * group + s] for q in range(parents)]
            for k in range(chunks):
                spectrum = ref[s * chunks + k].astype(F32)
                sre, sim = spectrum[:waves], spectrum[waves:]
                for q in range(parents):
                    gre = gains[q][0:1, k * 128 : (k + 1) * 128]
                    gim = gains[q][1:2, k * 128 : (k + 1) * 128]
                    at = (q * chunks + k) * 2
                    sums[at] = sums[at] + (gre * sre - gim * sim)
                    sums[at + 1] = sums[at + 1] + (gre * sim + gim * sre)
            return tuple(sums)

        sums = lax.fori_loop(0, group, add_source, sums, unroll=8)
    for q in range(parents):
        for k in range(chunks):
            at = (q * chunks + k) * 2
            re = sums[at].astype(BF16).astype(F32)
            im = sums[at + 1].astype(BF16).astype(F32)
            lanes = slice(k * 128, (k + 1) * 128)
            for c in range(8):
                cos, sin = cos_phase[c : c + 1, lanes], sin_phase[c : c + 1, lanes]
                rows = slice((q * 8 + c) * waves, (q * 8 + c + 1) * waves)
                down_re_ref[rows, lanes] = cos * re + sin * im
                down_im_ref[rows, lanes] = cos * im - sin * re
    imat = imat_ref[...]
    in_re = nt_dot(down_re_ref[...].astype(BF16), imat)
    in_im = nt_dot(down_im_ref[...].astype(BF16), imat)
    incoming = jnp.concatenate([in_re, in_im], axis=1).astype(BF16)
    far = nt_dot(incoming, rad_ref[...])
    factor = TURN * LEAD / math.sqrt(entries * width)
    out_ref[...] = sum_ref[...] * factor + far.reshape(near_ref.shape)


def per_device(
    currents, positions, radiation, interp_index, interp_weight, child_phase, near_src, trans_src, trans_id,
    trans_count, trans_table
):
    boxes, waves, width = currents.shape
    entries = near_src.shape[1]
    leaf_dirs = radiation.shape[1] // 2
    parent_dirs = child_phase.shape[1]
    parents = boxes // 8
    spectra_rows = parents * parent_dirs // 128
    size = lax.axis_size("dir")
    vmem = pl.BlockSpec(memory_space=pltpu.VMEM)
    smem = pl.BlockSpec(memory_space=pltpu.SMEM)
    hbm = pl.BlockSpec(memory_space=pltpu.HBM)
    params = pltpu.CompilerParams(vmem_limit_bytes=32 * 1024 * 1024)

    def in_hbm(x):
        return pltpu.with_memory_space_constraint(x, pltpu.HBM)

    def shaped(shape, dtype):
        return jax.ShapeDtypeStruct(shape, dtype)

    operands = (currents, positions.transpose(1, 0, 2), radiation, interp_index.T, interp_weight.T, child_phase)
    packet, spectra, imat, cos_phase, sin_phase, rad = pl.pallas_call(
        outgoing_kernel,
        out_shape=(
            shaped((boxes + spectra_rows, 16, width), BF16),
            shaped((spectra_rows, 2 * waves, 128), BF16),
            shaped((leaf_dirs, parent_dirs), BF16),
            shaped((8, parent_dirs), F32),
            shaped((8, parent_dirs), F32),
            shaped(radiation.shape, BF16),
        ),
        in_specs=[hbm] * len(operands),
        out_specs=(vmem,) * 6,
        scratch_shapes=[pltpu.VMEM(x.shape, x.dtype) for x in operands if x is not radiation]
        + [pltpu.SemaphoreType.DMA((len(operands),))],
        compiler_params=params,
        name="outgoing",
    )(*[in_hbm(x) for x in operands])

    steps = []
    for step in range(1, size):
        pairs = [(i, i ^ step) for i in range(size) if i < i ^ step]
        steps.append(swapped(packet if carries_packet(step) else spectra, "dir", pairs))

    length = list_places(boxes, entries)[2]
    window = 3 * trans_src.shape[0]
    near_scratch = [
        pltpu.VMEM((ITEMS, width, 2 * width), F32),
        pltpu.VMEM((ITEMS, width, 2 * width), F32),
        pltpu.VMEM((ITEMS, width, 2 * width), BF16),
        pltpu.VMEM((ITEMS, width, 2 * width), BF16),
    ]
    own_sum, items, observers, sources, gains = pl.pallas_call(
        own_near_kernel,
        out_shape=(
            shaped((boxes, waves, width), F32),
            shaped((1, length), jnp.int32),
            shaped((boxes, 16, width), BF16),
            shaped((boxes, width, 128), BF16),
            shaped((parents, window, 2, parent_dirs), F32),
        ),
        in_specs=[vmem] + [hbm] * 5,
        out_specs=(vmem,) * 5,
        scratch_shapes=[
            pltpu.VMEM(near_src.shape, jnp.int32),
            pltpu.SMEM((1, length), jnp.int32),
            pltpu.SMEM(trans_src.shape, jnp.int32),
            pltpu.SMEM(trans_id.shape, jnp.int32),
            pltpu.SMEM(trans_count.shape, jnp.int32),
            pltpu.VMEM((parents * trans_src.shape[1], 2, parent_dirs), F32),
        ]
        + near_scratch
        + [pltpu.SemaphoreType.DMA((4,))],
        compiler_params=params,
        name="own_near",
    )(packet, *[in_hbm(x) for x in (near_src, trans_src, trans_id, trans_count, trans_table)])

    group = pl.pallas_call(
        group_kernel,
        out_shape=shaped((size * spectra_rows + boxes, 2 * waves, 128), BF16),
        in_specs=[vmem] * (2 + len(steps)),
        out_specs=vmem,
        compiler_params=params,
        name="group",
    )(spectra, *steps, items)
    groups = lax.axis_size("box")
    group_even = swapped(group, "box", [(i, i + 1) for i in range(0, groups - 1, 2)])
    group_odd = swapped(group, "box", [(i, i + 1) for i in range(1, groups - 1, 2)])

    packets = [x for step, x in enumerate(steps, 1) if carries_packet(step)]
    near = pl.pallas_call(
        functools.partial(group_near_kernel, entries),
        out_shape=shaped((boxes, waves, width), F32),
        in_specs=[smem] + [vmem] * (4 + len(packets)),
        out_specs=vmem,
        scratch_shapes=[
            pltpu.VMEM((3 * boxes, 16, width), BF16),
            pltpu.VMEM((3 * boxes, width, 128), BF16),
        ]
        + near_scratch,
        compiler_params=params,
        name="group_near",
    )(items, packet, *packets, observers, sources, own_sum)

    return pl.pallas_call(
        functools.partial(incoming_kernel, entries),
        out_shape=shaped((boxes, waves, width), F32),
        in_specs=[smem] + [vmem] * 10,
        out_specs=vmem,
        scratch_shapes=[
            pltpu.VMEM((boxes, waves, width), F32),
            pltpu.VMEM((boxes, 16, width), BF16),
            pltpu.VMEM((boxes, width, 128), BF16),
            pltpu.VMEM((boxes * waves, parent_dirs), F32),
            pltpu.VMEM((boxes * waves, parent_dirs), F32),
        ]
        + near_scratch,
        compiler_params=params,
        name="incoming",
    )(items, group_even, group, group_odd, gains, cos_phase, sin_phase, imat, rad, observers, near)


def solution(mesh):
    placed = (
        P(("box", "dir"), None, None),
        P(("box", "dir"), None, None),
        P(),
        P(),
        P(),
        P(),
        P(("box", "dir"), None),
        P("box", None),
        P("box", None),
        P("box"),
        P(),
    )
    return jax.shard_map(
        per_device,
        mesh=mesh,
        in_specs=placed,
        out_specs=P(("box", "dir"), None, None),
        check_vma=False,
    )
```

profile of v0, /device:TPU:1, one launch (start us, length us, event | category | flops | bytes accessed | tf_op | source)
XLA Modules:
  0.0 34.2 jit_solution(17468791177361862095)
XLA Ops:
  0.0 1.3 %outgoing.1 = (bf16[24,16,128]{2,1,0:T(8,128)(2,1)S(1)}, bf16[8,16,128]{2,1,0:T(8,128)(2,1)S(1)}, bf16[128,512]{1,0:T(8,128)(2,1)S(1)}, f32[8,512]{1,0:T(8,128)S...) custom-call(bf16[16,8,128]{2,1,0:T(8,128)(2,1)} %x_hbm.1, bf16[3,16,128]{2,1,0:T(8,128)(2,1)} %bitcast.3, ...), custom_call_target="tpu_custom_call" | custom-call | tf_op jit(solution)/shard_map/outgoing/pallas_call | solution.py:467
  1.3 2.2 %collective-permute-start = (bf16[24,16,128]{2,1,0:T(8,128)(2,1)S(1)}, bf16[24,16,128]{2,1,0:T(8,128)(2,1)S(1)}, u32[]{:S(2)}, u32[]{:S(2)}) collective-permute-start(bf16[24,16,128]{2,1,0:T(8,128)(2,1)S(1)} %get-tuple-element.16.own_ref), channel_id=1, source_target_pairs={{0,1},{1,0},{2,3},{3,2},{4,5},{5,4},{6,7},{7,6},{8,9},{9,8},{10,11... | collective-permute-start | bytes 294920 | tf_op jit(solution)/shard_map/ppermute | solution.py:30
  3.5 2.2 %collective-permute-start.2 = (bf16[24,16,128]{2,1,0:T(8,128)(2,1)S(1)}, bf16[24,16,128]{2,1,0:T(8,128)(2,1)S(1)}, u32[]{:S(2)}, u32[]{:S(2)}) collective-permute-start(bf16[24,16,128]{2,1,0:T(8,128)(2,1)S(1)} %get-tuple-element.16.own_ref), channel_id=1, source_target_pairs={{0,3},{3,0},{1,2},{2,1},{4,7},{7,4},{5,6},{6,5},{8,11},{11,8},{9,1... | collective-permute-start | bytes 294920 | tf_op jit(solution)/shard_map/ppermute | solution.py:30
  5.7 0.1 collective-permute-start.1
  5.8 8.3 %own_near.1 = (f32[16,8,128]{2,1,0:T(8,128)S(1)}, s32[1,512]{1,0:T(1,128)S(1)}, bf16[16,16,128]{2,1,0:T(8,128)(2,1)S(1)}, bf16[16,128,128]{2,1,0:T(8,128)(2,1)S(1)}, f32[2,24,2,512]{3,2,1,0:T(2,128)S(1)}) custom-call(bf16[24,16,128]{2,1,0:T(8,128)(2,1)S(1)} %get-tuple-element.16.own_ref, s32[16,27]{1,0:T(8,128)} %near_hbm.1, s32[8,32]{1,0:T(8,128)} %src_hbm.1, ...), custom_call_target="tpu_custom_call" | custom-call | tf_op jit(solution)/shard_map/own_near/pallas_call | solution.py:498
  14.1 0.0 collective-permute-done.1.refs_1_
  14.1 0.0 collective-permute-done.refs_0_
  14.1 0.0 collective-permute-done.2.refs_2_.refs_1_
  14.2 2.0 %collective-permute-start.3 = (bf16[48,16,128]{2,1,0:T(8,128)(2,1)S(1)}, bf16[48,16,128]{2,1,0:T(8,128)(2,1)S(1)}, u32[]{:S(2)}, u32[]{:S(2)}) collective-permute-start(bf16[48,16,128]{2,1,0:T(8,128)(2,1)S(1)} %group.1.own_ref), channel_id=1, source_target_pairs={{0,4},{4,0},{8,12},{12,8},{16,20},{20,16},{24,28},{28,24},{1,5},{5... | collective-permute-start | bytes 589832 | tf_op jit(solution)/shard_map/ppermute | solution.py:30
  16.2 3.0 %collective-permute-start.4 = (bf16[48,16,128]{2,1,0:T(8,128)(2,1)S(1)}, bf16[48,16,128]{2,1,0:T(8,128)(2,1)S(1)}, u32[]{:S(2)}, u32[]{:S(2)}) collective-permute-start(bf16[48,16,128]{2,1,0:T(8,128)(2,1)S(1)} %group.1.own_ref), channel_id=1, source_target_pairs={{4,8},{8,4},{12,16},{16,12},{20,24},{24,20},{5,9},{9,5},{13,17},{1... | collective-permute-start | bytes 589832 | tf_op jit(solution)/shard_map/ppermute | solution.py:30
  19.2 7.3 %group_near.1.near_ref = f32[16,8,128]{2,1,0:T(8,128)S(1)} custom-call(s32[1,512]{1,0:T(1,128)S(1)} %get-tuple-element.17.refs_3_.items_ref, bf16[24,16,128]{2,1,0:T(8,128)(2,1)S(1)} %get-tuple-element.16.own_ref, bf16[24,16,128]{2,1,0:T(8,128)(2,1)S(1)} %collective-permute-done.refs_0_, bf16[24,16,128]{2,1,0:T(8,128)(2,1)S(1)} %collective-permute-done.2.refs_2_.refs_1_, ...), custom_call_target="tpu_custom_call" | custom-call | tf_op jit(solution)/shard_map/group_near/pallas_call | solution.py:536
  26.5 0.0 collective-permute-done.3.even_ref
  26.5 0.0 collective-permute-done.4.odd_ref
  26.5 7.7 %incoming.1 = f32[16,8,128]{2,1,0:T(8,128)} custom-call(s32[1,512]{1,0:T(1,128)S(1)} %get-tuple-element.17.refs_3_.items_ref, bf16[48,16,128]{2,1,0:T(8,128)(2,1)S(1)} %collective-permute-done.3.even_ref, bf16[48,16,128]{2,1,0:T(8,128)(2,1)S(1)} %group.1.own_ref, bf16[48,16,128]{2,1,0:T(8,128)(2,1)S(1)} %collective-permute-done.4.odd_ref, ...), custom_call_target="tpu_custom_call" | custom-call | tf_op jit(solution)/shard_map/incoming/pallas_call | solution.py:550
  (1 shorter events, 0.0 us)
Async XLA Ops:
  1.3 12.8 %collective-permute-start = (bf16[24,16,128]{2,1,0:T(8,128)(2,1)S(1)}, bf16[24,16,128]{2,1,0:T(8,128)(2,1)S(1)}, u32[]{:S(2)}, u32[]{:S(2)}) collective-permute-start(bf16[24,16,128]{2,1,0:T(8,128)(2,1)S(1)} %get-tuple-element.16.own_ref), channel_id=1, source_target_pairs={{0,1},{1,0},{2,3},{3,2},{4,5},{5,4},{6,7},{7,6},{8,9},{9,8},{10,11... | collective-permute-start | bytes 294920 | tf_op jit(solution)/shard_map/ppermute | solution.py:30
  3.5 10.6 %collective-permute-start.2 = (bf16[24,16,128]{2,1,0:T(8,128)(2,1)S(1)}, bf16[24,16,128]{2,1,0:T(8,128)(2,1)S(1)}, u32[]{:S(2)}, u32[]{:S(2)}) collective-permute-start(bf16[24,16,128]{2,1,0:T(8,128)(2,1)S(1)} %get-tuple-element.16.own_ref), channel_id=1, source_target_pairs={{0,3},{3,0},{1,2},{2,1},{4,7},{7,4},{5,6},{6,5},{8,11},{11,8},{9,1... | collective-permute-start | bytes 294920 | tf_op jit(solution)/shard_map/ppermute | solution.py:30
  5.7 8.4 %collective-permute-start.1 = (bf16[8,16,128]{2,1,0:T(8,128)(2,1)S(1)}, bf16[8,16,128]{2,1,0:T(8,128)(2,1)S(1)}, u32[]{:S(2)}, u32[]{:S(2)}) collective-permute-start(bf16[8,16,128]{2,1,0:T(8,128)(2,1)S(1)} %get-tuple-element.18.own_ref), channel_id=1, source_target_pairs={{0,2},{2,0},{1,3},{3,1},{4,6},{6,4},{5,7},{7,5},{8,10},{10,8},{9,1... | collective-permute-start | bytes 98312 | tf_op jit(solution)/shard_map/ppermute | solution.py:30
  14.2 12.4 %collective-permute-start.3 = (bf16[48,16,128]{2,1,0:T(8,128)(2,1)S(1)}, bf16[48,16,128]{2,1,0:T(8,128)(2,1)S(1)}, u32[]{:S(2)}, u32[]{:S(2)}) collective-permute-start(bf16[48,16,128]{2,1,0:T(8,128)(2,1)S(1)} %group.1.own_ref), channel_id=1, source_target_pairs={{0,4},{4,0},{8,12},{12,8},{16,20},{20,16},{24,28},{28,24},{1,5},{5... | collective-permute-start | bytes 589832 | tf_op jit(solution)/shard_map/ppermute | solution.py:30
  16.2 10.3 %collective-permute-start.4 = (bf16[48,16,128]{2,1,0:T(8,128)(2,1)S(1)}, bf16[48,16,128]{2,1,0:T(8,128)(2,1)S(1)}, u32[]{:S(2)}, u32[]{:S(2)}) collective-permute-start(bf16[48,16,128]{2,1,0:T(8,128)(2,1)S(1)} %group.1.own_ref), channel_id=1, source_target_pairs={{4,8},{8,4},{12,16},{16,12},{20,24},{24,20},{5,9},{9,5},{13,17},{1... | collective-permute-start | bytes 589832 | tf_op jit(solution)/shard_map/ppermute | solution.py:30
where the time goes:
time: 34.9 us; the launch traced here: 34.2 us
  Pallas kernels  24.6 us (70%)
  starting transfers between devices  9.57 us (27%)
    ppermute x5, starting transfers between devices, swapped(): lax.ppermute(x, axis, [way for i, j in pairs for way in ((i, j), (j, i))])  9.57 us
    pallas_call x1, Pallas kernels, per_device(): pl.pallas_call(own_near_kernel, out_shape=(shaped((boxes, waves, width),...  8.27 us
    pallas_call x1, Pallas kernels, per_device(): pl.pallas_call(functools.partial(incoming_kernel, entries), out_shape=sha...  7.72 us
    pallas_call x1, Pallas kernels, per_device(): pl.pallas_call(functools.partial(group_near_kernel, entries), out_shape=s...  7.28 us
    pallas_call x1, Pallas kernels, per_device(): pl.pallas_call(outgoing_kernel, out_shape=(shaped((boxes + spectra_rows,...  1.31 us
  transfers between devices with their start and end apart: 5, of which 0 were waited for; matrix products, arithmetic and copies ran while one was open for 0% of the time, Pallas kernels for 45%

commit v1 on v0

--- a/solution.py
+++ b/solution.py
@@ -16,7 +16,6 @@
 TURN = WAVENUMBER / (2.0 * math.pi)
 S0, S1, S2 = (-0.08849679958812066, 0.5822236432316782, -1.1456733260321648)
 LEAD = -70.99877392901621
-ROUNDER = 12582912.0
 ITEMS = 4
 ROWS = 32
 OWN_MOST = 4
@@ -252,7 +251,7 @@
         for at in range(0, width, ROWS):
             v = jnp.maximum(u_ref[g, at : at + ROWS], 1e-12)
             q = v * lax.rsqrt(v)
-            t = q - ((q + ROUNDER) - ROUNDER)
+            t = q - jnp.round(q)
             x = 0.25 - jnp.abs(t)
             z = x * x
             cosine = x * (((z + S2) * z + S1) * z + S0)

time: 34.9 us -> 34.5 us (0.989); the launches traced: 34.2 us -> 34.2 us
  starting transfers between devices: 9.57 us -> 8.81 us
  Pallas kernels: 24.6 us -> 25.3 us
    ppermute x5, starting transfers between devices: 9.57 us -> 8.81 us  [swapped(): lax.ppermute(x, axis, [way for i, j in pairs for way in ((i, j), (j, i))])]
    pallas_call x1, Pallas kernels: 7.72 us -> 8.21 us  [per_device(): pl.pallas_call(functools.partial(incoming_kernel, entries), out_shape=sha...]
    pallas_call x1, Pallas kernels: 8.27 us -> 8.71 us  [per_device(): pl.pallas_call(own_near_kernel, out_shape=(shaped((boxes, waves, width),...]
  transfers between devices with their start and end apart: 5 -> 5, of which waited for: 0 -> 0; matrix products, arithmetic and copies ran while one was open for 0% -> 0% of each run, Pallas kernels for 45% -> 46%
where the time goes in v1:
time: 34.5 us; the launch traced here: 34.2 us
  Pallas kernels  25.3 us (73%)
  starting transfers between devices  8.81 us (26%)
    ppermute x5, starting transfers between devices, swapped(): lax.ppermute(x, axis, [way for i, j in pairs for way in ((i, j), (j, i))])  8.81 us
    pallas_call x1, Pallas kernels, per_device(): pl.pallas_call(own_near_kernel, out_shape=(shaped((boxes, waves, width),...  8.71 us
    pallas_call x1, Pallas kernels, per_device(): pl.pallas_call(functools.partial(incoming_kernel, entries), out_shape=sha...  8.21 us
    pallas_call x1, Pallas kernels, per_device(): pl.pallas_call(functools.partial(group_near_kernel, entries), out_shape=s...  7.09 us
    pallas_call x1, Pallas kernels, per_device(): pl.pallas_call(outgoing_kernel, out_shape=(shaped((boxes + spectra_rows,...  1.31 us
  transfers between devices with their start and end apart: 5, of which 0 were waited for; matrix products, arithmetic and copies ran while one was open for 0% of the time, Pallas kernels for 46%

profile of v1, /device:TPU:1, one launch (start us, length us, event | category | flops | bytes accessed | tf_op | source)
XLA Modules:
  0.0 34.2 jit_solution(4606080691212503561)
XLA Ops:
  0.0 1.3 %outgoing.1 = (bf16[24,16,128]{2,1,0:T(8,128)(2,1)S(1)}, bf16[8,16,128]{2,1,0:T(8,128)(2,1)S(1)}, bf16[128,512]{1,0:T(8,128)(2,1)S(1)}, f32[8,512]{1,0:T(8,128)S...) custom-call(bf16[16,8,128]{2,1,0:T(8,128)(2,1)} %x_hbm.1, bf16[3,16,128]{2,1,0:T(8,128)(2,1)} %bitcast.3, ...), custom_call_target="tpu_custom_call" | custom-call | tf_op jit(solution)/shard_map/outgoing/pallas_call | solution.py:466
  1.3 2.2 %collective-permute-start = (bf16[24,16,128]{2,1,0:T(8,128)(2,1)S(1)}, bf16[24,16,128]{2,1,0:T(8,128)(2,1)S(1)}, u32[]{:S(2)}, u32[]{:S(2)}) collective-permute-start(bf16[24,16,128]{2,1,0:T(8,128)(2,1)S(1)} %get-tuple-element.16.own_ref), channel_id=1, source_target_pairs={{0,1},{1,0},{2,3},{3,2},{4,5},{5,4},{6,7},{7,6},{8,9},{9,8},{10,11... | collective-permute-start | bytes 294920 | tf_op jit(solution)/shard_map/ppermute | solution.py:29
  3.5 2.2 %collective-permute-start.2 = (bf16[24,16,128]{2,1,0:T(8,128)(2,1)S(1)}, bf16[24,16,128]{2,1,0:T(8,128)(2,1)S(1)}, u32[]{:S(2)}, u32[]{:S(2)}) collective-permute-start(bf16[24,16,128]{2,1,0:T(8,128)(2,1)S(1)} %get-tuple-element.16.own_ref), channel_id=1, source_target_pairs={{0,3},{3,0},{1,2},{2,1},{4,7},{7,4},{5,6},{6,5},{8,11},{11,8},{9,1... | collective-permute-start | bytes 294920 | tf_op jit(solution)/shard_map/ppermute | solution.py:29
  5.7 0.1 collective-permute-start.1
  5.8 8.7 %own_near.1 = (f32[16,8,128]{2,1,0:T(8,128)S(1)}, s32[1,512]{1,0:T(1,128)S(1)}, bf16[16,16,128]{2,1,0:T(8,128)(2,1)S(1)}, bf16[16,128,128]{2,1,0:T(8,128)(2,1)S(1)}, f32[2,24,2,512]{3,2,1,0:T(2,128)S(1)}) custom-call(bf16[24,16,128]{2,1,0:T(8,128)(2,1)S(1)} %get-tuple-element.16.own_ref, s32[16,27]{1,0:T(8,128)} %near_hbm.1, s32[8,32]{1,0:T(8,128)} %src_hbm.1, ...), custom_call_target="tpu_custom_call" | custom-call | tf_op jit(solution)/shard_map/own_near/pallas_call | solution.py:497
  14.5 0.0 collective-permute-done.1.refs_1_
  14.5 0.0 collective-permute-done.refs_0_
  14.6 0.0 collective-permute-done.2.refs_2_.refs_1_
  14.6 1.3 %collective-permute-start.3 = (bf16[48,16,128]{2,1,0:T(8,128)(2,1)S(1)}, bf16[48,16,128]{2,1,0:T(8,128)(2,1)S(1)}, u32[]{:S(2)}, u32[]{:S(2)}) collective-permute-start(bf16[48,16,128]{2,1,0:T(8,128)(2,1)S(1)} %group.1.own_ref), channel_id=1, source_target_pairs={{0,4},{4,0},{8,12},{12,8},{16,20},{20,16},{24,28},{28,24},{1,5},{5... | collective-permute-start | bytes 589832 | tf_op jit(solution)/shard_map/ppermute | solution.py:29
  15.9 3.1 %collective-permute-start.4 = (bf16[48,16,128]{2,1,0:T(8,128)(2,1)S(1)}, bf16[48,16,128]{2,1,0:T(8,128)(2,1)S(1)}, u32[]{:S(2)}, u32[]{:S(2)}) collective-permute-start(bf16[48,16,128]{2,1,0:T(8,128)(2,1)S(1)} %group.1.own_ref), channel_id=1, source_target_pairs={{4,8},{8,4},{12,16},{16,12},{20,24},{24,20},{5,9},{9,5},{13,17},{1... | collective-permute-start | bytes 589832 | tf_op jit(solution)/shard_map/ppermute | solution.py:29
  18.9 7.1 %group_near.1.near_ref = f32[16,8,128]{2,1,0:T(8,128)S(1)} custom-call(s32[1,512]{1,0:T(1,128)S(1)} %get-tuple-element.17.refs_3_.items_ref, bf16[24,16,128]{2,1,0:T(8,128)(2,1)S(1)} %get-tuple-element.16.own_ref, bf16[24,16,128]{2,1,0:T(8,128)(2,1)S(1)} %collective-permute-done.refs_0_, bf16[24,16,128]{2,1,0:T(8,128)(2,1)S(1)} %collective-permute-done.2.refs_2_.refs_1_, ...), custom_call_target="tpu_custom_call" | custom-call | tf_op jit(solution)/shard_map/group_near/pallas_call | solution.py:535
  26.0 0.0 collective-permute-done.3.even_ref
  26.0 0.0 collective-permute-done.4.odd_ref
  26.0 8.2 %incoming.1 = f32[16,8,128]{2,1,0:T(8,128)} custom-call(s32[1,512]{1,0:T(1,128)S(1)} %get-tuple-element.17.refs_3_.items_ref, bf16[48,16,128]{2,1,0:T(8,128)(2,1)S(1)} %collective-permute-done.3.even_ref, bf16[48,16,128]{2,1,0:T(8,128)(2,1)S(1)} %group.1.own_ref, bf16[48,16,128]{2,1,0:T(8,128)(2,1)S(1)} %collective-permute-done.4.odd_ref, ...), custom_call_target="tpu_custom_call" | custom-call | tf_op jit(solution)/shard_map/incoming/pallas_call | solution.py:549
  (1 shorter events, 0.0 us)
Async XLA Ops:
  1.3 13.2 %collective-permute-start = (bf16[24,16,128]{2,1,0:T(8,128)(2,1)S(1)}, bf16[24,16,128]{2,1,0:T(8,128)(2,1)S(1)}, u32[]{:S(2)}, u32[]{:S(2)}) collective-permute-start(bf16[24,16,128]{2,1,0:T(8,128)(2,1)S(1)} %get-tuple-element.16.own_ref), channel_id=1, source_target_pairs={{0,1},{1,0},{2,3},{3,2},{4,5},{5,4},{6,7},{7,6},{8,9},{9,8},{10,11... | collective-permute-start | bytes 294920 | tf_op jit(solution)/shard_map/ppermute | solution.py:29
  3.5 11.1 %collective-permute-start.2 = (bf16[24,16,128]{2,1,0:T(8,128)(2,1)S(1)}, bf16[24,16,128]{2,1,0:T(8,128)(2,1)S(1)}, u32[]{:S(2)}, u32[]{:S(2)}) collective-permute-start(bf16[24,16,128]{2,1,0:T(8,128)(2,1)S(1)} %get-tuple-element.16.own_ref), channel_id=1, source_target_pairs={{0,3},{3,0},{1,2},{2,1},{4,7},{7,4},{5,6},{6,5},{8,11},{11,8},{9,1... | collective-permute-start | bytes 294920 | tf_op jit(solution)/shard_map/ppermute | solution.py:29
  5.7 8.8 %collective-permute-start.1 = (bf16[8,16,128]{2,1,0:T(8,128)(2,1)S(1)}, bf16[8,16,128]{2,1,0:T(8,128)(2,1)S(1)}, u32[]{:S(2)}, u32[]{:S(2)}) collective-permute-start(bf16[8,16,128]{2,1,0:T(8,128)(2,1)S(1)} %get-tuple-element.18.own_ref), channel_id=1, source_target_pairs={{0,2},{2,0},{1,3},{3,1},{4,6},{6,4},{5,7},{7,5},{8,10},{10,8},{9,1... | collective-permute-start | bytes 98312 | tf_op jit(solution)/shard_map/ppermute | solution.py:29
  14.6 11.4 %collective-permute-start.3 = (bf16[48,16,128]{2,1,0:T(8,128)(2,1)S(1)}, bf16[48,16,128]{2,1,0:T(8,128)(2,1)S(1)}, u32[]{:S(2)}, u32[]{:S(2)}) collective-permute-start(bf16[48,16,128]{2,1,0:T(8,128)(2,1)S(1)} %group.1.own_ref), channel_id=1, source_target_pairs={{0,4},{4,0},{8,12},{12,8},{16,20},{20,16},{24,28},{28,24},{1,5},{5... | collective-permute-start | bytes 589832 | tf_op jit(solution)/shard_map/ppermute | solution.py:29
  15.9 10.2 %collective-permute-start.4 = (bf16[48,16,128]{2,1,0:T(8,128)(2,1)S(1)}, bf16[48,16,128]{2,1,0:T(8,128)(2,1)S(1)}, u32[]{:S(2)}, u32[]{:S(2)}) collective-permute-start(bf16[48,16,128]{2,1,0:T(8,128)(2,1)S(1)} %group.1.own_ref), channel_id=1, source_target_pairs={{4,8},{8,4},{12,16},{16,12},{20,24},{24,20},{5,9},{9,5},{13,17},{1... | collective-permute-start | bytes 589832 | tf_op jit(solution)/shard_map/ppermute | solution.py:29
